TPU v7x, 512 devices: a whole 4x4x16 slice. The times are simulated.
512 devices in a mesh: space: 32 (over z, x_lo), member: 16 (over x_hi, y, core).
Axes of the slice: x: 4 (x_hi: 2, x_lo: 2; x = x_hi * 2 + x_lo), y: 4, z: 16, core: 2. Of those that a mesh axis runs over, the one named last changes fastest.
Arguments:
- prediction_maps: bfloat16 [16, 72, 64, 1440], P('member', None, 'space'), may hold values from -6 to 6
- truth_analysis: float32 [72, 92160], P(None, ('space', 'member')), may hold values from -6 to 6
- reciprocal_spread: float32 [72], replicated, may hold values from 0.3 to 3
- deconv_inputs: bfloat16 [16, 72, 64, 1440], P('member', None, 'space'), may hold values from -6 to 6
- filter_tensor: bfloat16 [5, 5, 72, 72], replicated, may hold values from -0.125 to 0.125
Outputs:
- grad_hidden: bfloat16 [16, 72, 64, 1440], P('member', None, 'space')
- grad_kernel: float32 [5, 5, 72, 72], replicated
All inputs are finite; a program needn't handle non-finite values.
Results may differ from a plain program's by a relative error of at most 0.018.
Values may be sent and summed in bfloat16 or wider, within the bound.
A program may use at most 64 MiB of HBM per device.

v0:
```python
import functools

import jax
import jax.numpy as jnp
import numpy as np
from jax import lax
from jax.experimental import pallas as pl
from jax.experimental.pallas import tpu as pltpu
from jax.sharding import PartitionSpec as P

F32 = jnp.float32
BF16 = jnp.bfloat16
SPACE = 32
MEMBER = 16
CH = 72
CP = 80
LON = 1440
LP = 1536
PX = 180
KW = 5
KC = KW * CP
PK = 112
TILES = 9


def reducer_step(t, m):
    return lax.rem(t + 62 - 16 * lax.rem(m, 2), SPACE)


def is_reducer(t, m):
    u = reducer_step(t, m)
    return jnp.logical_and(lax.rem(u, 3) == 0, u <= 3 * (TILES - 1))


def reducer_of(j, m):
    return lax.rem(3 * j + 2 + 16 * lax.rem(m, 2), SPACE)


def lane_index(rows):
    return lax.broadcasted_iota(jnp.int32, (rows, 128), 1)


def packed(wide):
    lane = lane_index(40)
    rest = wide[:, 128:256]
    low = rest[0:40]
    high = jnp.concatenate([rest[40:72], jnp.zeros((8, 128), F32)], axis=0)
    low = jnp.where(lane < PX - 128, low, 0.0)
    high = jnp.where(lane < PX - 128, high, 0.0)
    tail = jnp.where(lane < 64, low, pltpu.roll(high, 64, 1))
    return jnp.concatenate([wide[:, 0:128], tail], axis=0)


def kernel(
    weight_ref,
    pred_ref,
    truth_ref,
    scale_ref,
    hidden_ref,
    filter_ref,
    back_ref,
    kgrad_ref,
    send1,
    recv1,
    scaled,
    trscr,
    fscr,
    send2,
    recv2,
    ext,
    stack,
    wst,
    gka,
    total,
    out_acc,
    ar1_send,
    ar1_recv,
    ar2_send,
    ar2_recv,
    ar3_send,
    ar3_recv,
    ar4_send,
    ar4_recv,
    s1_sem,
    r1_sem,
    s2_sem,
    r2_sem,
    a1_ssem,
    a1_rsem,
    a2_ssem,
    a2_rsem,
    a3_ssem,
    a3_rsem,
    a4_ssem,
    a4_rsem,
):
    s = lax.axis_index("space")
    m = lax.axis_index("member")
    has_prev = s > 0
    has_next = s < SPACE - 1
    reducing = is_reducer(s, m)

    barrier = pltpu.get_barrier_semaphore()

    def greet(space, member):
        pl.semaphore_signal(barrier, inc=1, device_id={"space": space, "member": member})

    def greet_members(d, _):
        greet(s, lax.rem(m + d, MEMBER))
        return 0

    lax.fori_loop(1, MEMBER, greet_members, 0)

    def greet_bands(d, _):
        n = lax.rem(m + d, MEMBER)

        @pl.when(has_prev)
        def _():
            greet(s - 1, n)

        @pl.when(has_next)
        def _():
            greet(s + 1, n)

        return 0

    lax.fori_loop(0, MEMBER, greet_bands, 0)

    def greet_reducers(d, _):
        t = lax.rem(s + d, SPACE)

        @pl.when(jnp.logical_or(reducing, is_reducer(t, m)))
        def _():
            greet(t, m)

        return 0

    lax.fori_loop(1, SPACE, greet_reducers, 0)
    pl.semaphore_wait(
        barrier,
        MEMBER
        - 1
        + jnp.where(has_prev, MEMBER, 0)
        + jnp.where(has_next, MEMBER, 0)
        + jnp.where(reducing, SPACE - 1, TILES),
    )

    def copy1(src, slot, member):
        return pltpu.make_async_remote_copy(
            src_ref=send1.at[src],
            dst_ref=recv1.at[slot],
            send_sem=s1_sem.at[src],
            recv_sem=r1_sem.at[slot],
            device_id={"space": s, "member": member},
        )

    def fields_out(d, _):
        n = lax.rem(m + d, MEMBER)
        row = n // 8
        start = PX * lax.rem(n, 8)
        off = lax.rem(start, 128)
        base = pl.multiple_of(start - off, 128)
        window = pred_ref[row, :, pl.ds(base, 384)].astype(F32)
        wide = pltpu.roll(window, lax.rem(384 - off, 384), 1)[:, 0:256]
        chunk = packed(wide).astype(BF16)

        @pl.when(d < MEMBER)
        def _():
            send1[n] = chunk
            copy1(n, m, n).start()

        @pl.when(d == MEMBER)
        def _():
            recv1[n] = chunk

        return 0

    lax.fori_loop(1, MEMBER + 1, fields_out, 0)

    eye = lax.broadcasted_iota(jnp.int32, (CH, CH), 0) == lax.broadcasted_iota(jnp.int32, (CH, CH), 1)
    scale_col = jnp.sum(jnp.where(eye, scale_ref[...], 0.0), axis=1, keepdims=True)
    lane40 = lane_index(40)
    scale_wide = jnp.broadcast_to(scale_col, (CH, 128))
    scale_pk = packed(jnp.concatenate([scale_wide, scale_wide], axis=1))
    trscr[...] = jnp.zeros_like(trscr)
    trscr[:, 0:PX] = truth_ref[...]
    truth_pk = packed(trscr[...])

    fscr[...] = jnp.zeros_like(fscr)
    wst[...] = jnp.zeros_like(wst)
    for a in range(KW):
        acc = None
        for b in range(KW):
            fscr[0:CH, 0:CH] = filter_ref[a, b].astype(F32)
            part = jnp.concatenate([fscr[...], jnp.zeros((CP, 384), F32)], axis=1)
            if b:
                part = pltpu.roll(part, CP * b, 1)
            acc = part if acc is None else acc + part
        acc = acc.astype(BF16)
        wst[a, 0:CP, :] = acc
        wst[a + 1, CP : 2 * CP, :] = acc
    gka[...] = jnp.zeros_like(gka)
    out_acc[...] = jnp.zeros_like(out_acc)

    def fields_in(d, _):
        n = lax.rem(m + MEMBER - d, MEMBER)

        @pl.when(d < MEMBER)
        def _():
            copy1(n, n, n).wait_recv()

        scaled[n] = scale_pk * recv1[n].astype(F32)
        return 0

    lax.fori_loop(1, MEMBER + 1, fields_in, 0)

    weight = weight_ref[2 * s + m // 8]

    def copy2(kind, src, slot, space, member):
        return pltpu.make_async_remote_copy(
            src_ref=send2.at[src],
            dst_ref=recv2.at[kind, slot],
            send_sem=s2_sem.at[kind, src],
            recv_sem=r2_sem.at[kind, slot],
            device_id={"space": space, "member": member},
        )

    def column_sums(square):
        main = jnp.sum(square[0:CH], axis=0, keepdims=True)
        tail = jnp.sum(square[CH:PK], axis=0, keepdims=True)
        return main, tail + pltpu.roll(tail, 64, 1)

    def spread_out(main, tail):
        return jnp.concatenate(
            [jnp.broadcast_to(main, (CH, 128)), jnp.broadcast_to(tail, (PK - CH, 128))], axis=0
        )

    def gradient(d, _):
        n = lax.rem(m + d, MEMBER)
        y = scaled[n]
        offset = scale_pk * (recv1[n].astype(F32) - truth_pk)
        main, tail = column_sums(offset * offset)
        direct = scale_pk * offset * spread_out(lax.rsqrt(main + 1.0), lax.rsqrt(tail + 1.0))

        def pair(k, mix):
            diff = scaled[k] - y
            main, tail = column_sums(diff * diff)
            return mix + diff * spread_out(lax.rsqrt(main + 1.0), lax.rsqrt(tail + 1.0))

        mix = lax.fori_loop(0, MEMBER, pair, jnp.zeros((PK, 128), F32), unroll=4)
        grad = (weight * (direct + scale_pk * mix * (1.0 / MEMBER))).astype(BF16)
        send2[n] = grad

        @pl.when(d < MEMBER)
        def _():
            copy2(1, n, m, s, n).start()

        @pl.when(d == MEMBER)
        def _():
            recv2[1, n] = grad

        return 0

    lax.fori_loop(1, MEMBER + 1, gradient, 0)

    def halo_prev(d, _):
        n = lax.rem(m + d, MEMBER)

        @pl.when(has_prev)
        def _():
            copy2(2, n, m, s - 1, n).start()

        return 0

    def halo_next(d, _):
        n = lax.rem(m + d, MEMBER)

        @pl.when(has_next)
        def _():
            copy2(0, n, m, s + 1, n).start()

        return 0

    lax.fori_loop(0, MEMBER, halo_prev, 0)
    lax.fori_loop(0, MEMBER, halo_next, 0)

    def wait_block(kind):
        def one(d, _):
            n = lax.rem(m + MEMBER - d, MEMBER)

            @pl.when(jnp.logical_or(kind != 1, d > 0))
            def _():
                copy2(kind, n, n, s, n).wait_recv()

            return 0

        lax.fori_loop(0, MEMBER, one, 0)

    def rows_ready(kind, half):
        q = 2 * kind + half
        ext[...] = jnp.zeros_like(ext)
        lane = lane40
        for k in range(8):
            chunk = recv2[kind, 8 * half + k].astype(F32)
            tail = chunk[CH:PK]
            low = jnp.where(lane < PX - 128, tail, 0.0)
            high = jnp.where(lane < PX - 128, pltpu.roll(tail, 64, 1), 0.0)
            rest = jnp.concatenate([low, high[0:32]], axis=0)
            wide = jnp.concatenate([chunk[0:CH], rest, jnp.zeros((CH, 128), F32)], axis=1)
            start = PX * k + 2
            base, off = start // 128 * 128, start % 128
            ext[0:CH, base : base + 384] += pltpu.roll(wide, off, 1)
        first = ext[:, 0:128]
        last = ext[:, LP - 128 : LP]
        lane80 = lane_index(CP)
        ext[:, 0:128] = jnp.where(lane80 < 2, pltpu.roll(last, 96, 1), first)
        ext[:, LP - 128 : LP] = jnp.where(
            jnp.logical_and(lane80 >= 34, lane80 < 36), pltpu.roll(first, 32, 1), last
        )
        for g in range(CP // 16):
            rows = ext[16 * g : 16 * g + 16, :]
            for b in range(KW):
                moved = rows if b == 0 else pltpu.roll(rows, LP - b, 1)
                at = pl.multiple_of((KW * q + b) * CP + 16 * g, 16)
                stack[pl.ds(at, 16), :] = moved.astype(BF16)

    def stacked(q):
        return stack[pl.ds(pl.multiple_of(q * KC, 16), KC), :]

    def kernel_terms(q):
        product = lax.dot_general(
            hidden_ref[...], stacked(q), (((1,), (1,)), ((), ())), preferred_element_type=F32
        )
        up = jnp.minimum(q, KW - 1)
        down = jnp.maximum(q - 1, 0)

        @pl.when(q < KW)
        def _():
            gka[up, :, 0:KC] += product[0:CP]

        @pl.when(q > 0)
        def _():
            gka[down, :, 0:KC] += product[CP : 2 * CP]

    def hidden_terms(q):
        out_acc[...] += jnp.dot(wst[q, :, 0:KC], stacked(q), preferred_element_type=F32)

    def present(kind):
        return jnp.logical_and(
            jnp.logical_or(kind != 0, has_prev), jnp.logical_or(kind != 2, has_next)
        )

    def block(i, _):
        kind = lax.rem(i + 1, 3)

        @pl.when(present(kind))
        def _():
            wait_block(kind)

            def half_step(half, _):
                rows_ready(kind, half)
                kernel_terms(2 * kind + half)

                @pl.when(i < 2)
                def _():
                    hidden_terms(2 * kind + half)

                return 0

            lax.fori_loop(0, 2, half_step, 0)

        return 0

    lax.fori_loop(0, 3, block, 0)

    total[...] = jnp.zeros_like(total)
    for a in range(KW):
        base, off = KC * a // 128 * 128, KC * a % 128
        part = gka[a]
        total[:, base : base + 512] += pltpu.roll(part, off, 1) if off else part

    def copy_a1(src, slot, member):
        return pltpu.make_async_remote_copy(
            src_ref=ar1_send.at[src],
            dst_ref=ar1_recv.at[slot],
            send_sem=a1_ssem.at[src],
            recv_sem=a1_rsem.at[slot],
            device_id={"space": s, "member": member},
        )

    def shares_out(d, _):
        n = lax.rem(m + d, MEMBER)
        ar1_send[n] = total[:, pl.ds(pl.multiple_of(128 * n, 128), 128)].astype(BF16)
        copy_a1(n, m, n).start()
        return 0

    lax.fori_loop(1, MEMBER, shares_out, 0)

    @pl.when(has_prev)
    def _():
        hidden_terms(0)
        hidden_terms(1)

    back_ref[0] = out_acc[0:CH, 0:LON].astype(BF16)
    back_ref[1] = out_acc[CP : CP + CH, 0:LON].astype(BF16)

    def shares_in(d, acc):
        n = lax.rem(m + MEMBER - d, MEMBER)
        copy_a1(n, n, n).wait_recv()
        return acc + ar1_recv[n].astype(F32)

    own = total[:, pl.ds(pl.multiple_of(128 * m, 128), 128)]
    share = lax.fori_loop(1, MEMBER, shares_in, own)

    for j in range(TILES):
        ar2_send[j] = share[8 * j : 8 * j + 8]

    def copy_a2(j, slot, space):
        return pltpu.make_async_remote_copy(
            src_ref=ar2_send.at[j],
            dst_ref=ar2_recv.at[slot],
            send_sem=a2_ssem.at[j],
            recv_sem=a2_rsem.at[slot],
            device_id={"space": space, "member": m},
        )

    def tiles_out(j, _):
        t = reducer_of(j, m)

        @pl.when(t != s)
        def _():
            copy_a2(j, s, t).start()

        return 0

    lax.fori_loop(0, TILES, tiles_out, 0)
    mine = jnp.minimum(reducer_step(s, m) // 3, TILES - 1)
    norm = float(1.0 / np.sqrt(np.float32(MEMBER * 2 * SPACE * LON)))

    def copy_a3(j, t, space):
        return pltpu.make_async_remote_copy(
            src_ref=ar3_send,
            dst_ref=ar3_recv.at[j],
            send_sem=a3_ssem.at[t],
            recv_sem=a3_rsem.at[j],
            device_id={"space": space, "member": m},
        )

    @pl.when(reducing)
    def _():
        def tiles_in(d, acc):
            t = lax.rem(s + SPACE - d, SPACE)
            copy_a2(0, t, t).wait_recv()
            return acc + ar2_recv[t]

        tile = lax.fori_loop(1, SPACE, tiles_in, ar2_send[mine]) * norm
        ar3_send[...] = tile
        ar3_recv[mine] = tile

        def tile_to(d, _):
            t = lax.rem(s + d, SPACE)
            copy_a3(mine, t, t).start()
            return 0

        lax.fori_loop(1, SPACE, tile_to, 0)

    def tiles_back(j, _):
        t = reducer_of(j, m)

        @pl.when(t != s)
        def _():
            copy_a3(j, 0, t).wait_recv()

        return 0

    lax.fori_loop(0, TILES, tiles_back, 0)

    final = jnp.concatenate([ar3_recv[j] for j in range(TILES)] + [jnp.zeros((8, 128), F32)], axis=0)
    ar4_send[...] = final.astype(BF16)
    total[:, pl.ds(pl.multiple_of(128 * m, 128), 128)] = final

    def copy_a4(n, slot, member):
        return pltpu.make_async_remote_copy(
            src_ref=ar4_send,
            dst_ref=ar4_recv.at[slot],
            send_sem=a4_ssem.at[n],
            recv_sem=a4_rsem.at[slot],
            device_id={"space": s, "member": member},
        )

    def totals_out(d, _):
        n = lax.rem(m + d, MEMBER)
        copy_a4(n, m, n).start()
        return 0

    lax.fori_loop(1, MEMBER, totals_out, 0)
    total[:, pl.ds(pl.multiple_of(128 * m, 128), 128)] = final.astype(BF16).astype(F32)

    def totals_in(d, _):
        n = lax.rem(m + MEMBER - d, MEMBER)
        copy_a4(n, n, n).wait_recv()
        total[:, pl.ds(pl.multiple_of(128 * n, 128), 128)] = ar4_recv[n].astype(F32)
        return 0

    lax.fori_loop(1, MEMBER, totals_in, 0)
    for k in range(KW * KW):
        base, off = CP * k // 128 * 128, CP * k % 128
        width = 256 if off else 128
        part = total[0:CH, base : base + width]
        if off:
            part = pltpu.roll(part, width - off, 1)
        kgrad_ref[k] = part[:, 0:CH]

    def sent(d, _):
        n = lax.rem(m + d, MEMBER)
        copy1(n, m, n).wait_send()
        copy2(1, n, m, s, n).wait_send()
        copy_a1(n, m, n).wait_send()
        copy_a4(n, m, n).wait_send()
        return 0

    lax.fori_loop(1, MEMBER, sent, 0)

    def halo_sent(d, _):
        n = lax.rem(m + d, MEMBER)

        @pl.when(has_prev)
        def _():
            copy2(2, n, m, s - 1, n).wait_send()

        @pl.when(has_next)
        def _():
            copy2(0, n, m, s + 1, n).wait_send()

        return 0

    lax.fori_loop(0, MEMBER, halo_sent, 0)

    def tiles_sent(j, _):
        t = reducer_of(j, m)

        @pl.when(t != s)
        def _():
            copy_a2(j, s, t).wait_send()

        return 0

    lax.fori_loop(0, TILES, tiles_sent, 0)

    @pl.when(reducing)
    def _():
        def one(d, _):
            t = lax.rem(s + d, SPACE)
            copy_a3(mine, t, t).wait_send()
            return 0

        lax.fori_loop(1, SPACE, one, 0)


def call(weights, pred, truth, scale, hidden, filters):
    vmem = pl.BlockSpec(memory_space=pltpu.VMEM)
    dma = pltpu.SemaphoreType.DMA
    return pl.pallas_call(
        kernel,
        out_shape=(
            jax.ShapeDtypeStruct((2, CH, LON), BF16),
            jax.ShapeDtypeStruct((KW * KW, CH, CH), F32),
        ),
        in_specs=[pl.BlockSpec(memory_space=pltpu.SMEM)] + [vmem] * 5,
        out_specs=(vmem, vmem),
        scratch_shapes=[
            pltpu.VMEM((MEMBER, PK, 128), BF16),
            pltpu.VMEM((MEMBER, PK, 128), BF16),
            pltpu.VMEM((MEMBER, PK, 128), F32),
            pltpu.VMEM((CH, 256), F32),
            pltpu.VMEM((CP, 128), F32),
            pltpu.VMEM((MEMBER, PK, 128), BF16),
            pltpu.VMEM((3, MEMBER, PK, 128), BF16),
            pltpu.VMEM((CP, LP), F32),
            pltpu.VMEM((6 * KC, LP), BF16),
            pltpu.VMEM((6, 2 * CP, 512), BF16),
            pltpu.VMEM((KW, CP, 512), F32),
            pltpu.VMEM((CP, 2048), F32),
            pltpu.VMEM((2 * CP, LP), F32),
            pltpu.VMEM((MEMBER, CP, 128), BF16),
            pltpu.VMEM((MEMBER, CP, 128), BF16),
            pltpu.VMEM((TILES, 8, 128), F32),
            pltpu.VMEM((SPACE, 8, 128), F32),
            pltpu.VMEM((8, 128), F32),
            pltpu.VMEM((TILES, 8, 128), F32),
            pltpu.VMEM((CP, 128), BF16),
            pltpu.VMEM((MEMBER, CP, 128), BF16),
            dma((MEMBER,)),
            dma((MEMBER,)),
            dma((3, MEMBER)),
            dma((3, MEMBER)),
            dma((MEMBER,)),
            dma((MEMBER,)),
            dma((TILES,)),
            dma((SPACE,)),
            dma((SPACE,)),
            dma((TILES,)),
            dma((MEMBER,)),
            dma((MEMBER,)),
        ],
        compiler_params=pltpu.CompilerParams(
            collective_id=0, has_side_effects=True, vmem_limit_bytes=48 * 1024 * 1024
        ),
    )(weights, pred, truth, scale, hidden, filters)


def body(prediction_maps, truth_analysis, reciprocal_spread, deconv_inputs, filter_tensor):
    rows = 2 * SPACE
    index = np.arange(rows, dtype=np.float64)
    cosine = np.cos((index + 0.5) * (np.pi / rows) - np.pi / 2)
    weights = jnp.asarray((cosine / cosine.mean()).astype(np.float32))
    pred = jnp.pad(jnp.transpose(prediction_maps[0], (1, 0, 2)), ((0, 0), (0, 0), (0, LP - LON)))
    hidden = jnp.pad(
        jnp.transpose(deconv_inputs[0], (1, 0, 2)), ((0, 0), (0, CP - CH), (0, LP - LON))
    ).reshape(2 * CP, LP)
    back, kgrad = call(
        weights, pred, truth_analysis, reciprocal_spread.reshape(1, CH), hidden, filter_tensor
    )
    return jnp.transpose(back, (1, 0, 2))[None], kgrad.reshape(KW, KW, CH, CH)


def solution(mesh):
    return jax.shard_map(
        body,
        mesh=mesh,
        in_specs=(
            P("member", None, "space", None),
            P(None, ("space", "member")),
            P(),
            P("member", None, "space", None),
            P(),
        ),
        out_specs=(P("member", None, "space", None), P()),
        check_vma=False,
    )
```

profile of v0, /device:TPU:1, one launch (start us, length us, event | category | flops | bytes accessed | tf_op | source)
XLA Modules:
  0.0 95.1 jit_solution(1479952527926830932)
XLA Ops:
  0.6 1.1 %copy.13 = bf16[1,72,2,1440]{3,1,2,0:T(8,128)(2,1)S(1)} copy(bf16[1,72,2,1440]{3,2,1,0:T(2,128)(2,1)} %param.6) | data formatting | bytes 829440 | tf_op args[0]
  1.7 0.0 copy-start.4
  1.7 1.0 %copy-done.4 = bf16[1,72,2,1440]{3,2,1,0:T(2,128)(2,1)S(1)} copy-done((bf16[1,72,2,1440]{3,2,1,0:T(2,128)(2,1)S(1)}, bf16[1,72,2,1440]{3,2,1,0:T(2,128)(2,1)}, u32[]{:S(2)}) %copy-start.4) | copy-done | bytes 414744
  2.8 0.0 copy-start
  2.8 0.0 copy-start.1
  2.8 0.0 copy-start.2
  2.8 0.0 copy-start.3
  2.9 0.9 copy-done
  3.8 0.0 copy-done.1
  3.8 0.0 copy-done.2
  3.8 0.0 copy-done.3
  3.8 89.3 %shard_map.77 = (bf16[2,72,1440]{2,1,0:T(8,128)(2,1)S(1)}, f32[25,72,72]{2,1,0:T(8,128)S(1)}) custom-call(f32[64]{0:T(128)S(1)} %copy-done.3, bf16[2,72,1536]{2,1,0:T(8,128)(2,1)S(1)} %pad.8.pred_ref, f32[72,180]{1,0:T(8,128)S(1)} %copy-done.1, f32[1,72]{1,0:T(1,128)S(1)} %bitcast.17, bf16[160,1536]{1,0:T(8,128)(2,1)S(1)} %bitcast.14, ...), custom_call_target="tpu_custom_call" | custom-call | tf_op jit(solution)/shard_map/pallas_call | solution.py:563
  93.1 1.1 %copy.10 = bf16[1,72,2,1440]{3,2,1,0:T(2,128)(2,1)} copy(bf16[1,72,2,1440]{3,1,2,0:T(8,128)(2,1)S(1)} %bitcast.16) | data formatting | bytes 829440
  94.2 0.9 copy.15
  (3 shorter events, 0.1 us)
Async XLA Ops:
  1.7 1.0 %copy-start.4 = (bf16[1,72,2,1440]{3,2,1,0:T(2,128)(2,1)S(1)}, bf16[1,72,2,1440]{3,2,1,0:T(2,128)(2,1)}, u32[]{:S(2)}) copy-start(bf16[1,72,2,1440]{3,2,1,0:T(2,128)(2,1)} %param.9) | copy-start | bytes 1244164
  2.8 1.0 %copy-start = (bf16[5,5,72,72]{3,2,1,0:T(8,128)(2,1)S(1)}, bf16[5,5,72,72]{3,2,1,0:T(8,128)(2,1)}, u32[]{:S(2)}) copy-start(bf16[5,5,72,72]{3,2,1,0:T(8,128)(2,1)} %filter_ref.1) | copy-start | bytes 777604
  2.8 1.0 %copy-start.1 = (f32[72,180]{1,0:T(8,128)S(1)}, f32[72,180]{1,0:T(8,128)}, u32[]{:S(2)}) copy-start(f32[72,180]{1,0:T(8,128)} %truth_ref.1) | copy-start | bytes 155524
  2.8 1.0 %copy-start.2 = (f32[72]{0:T(128)S(1)}, f32[72]{0:T(128)}, u32[]{:S(2)}) copy-start(f32[72]{0:T(128)} %param.8) | copy-start | bytes 868
  2.8 0.9 copy-start.3
where the time goes:
time: 95.3 us; the launch traced here: 95.1 us
  Pallas kernels  89.3 us (94%)
  local copies, waits for them, and re-layouts  5.12 us (5%)
    pallas_call x1, Pallas kernels, call(): pl.pallas_call(kernel, out_shape=(jax.ShapeDtypeStruct((2, CH, LON), BF16...  89.3 us
    unnamed x14, local copies, waits for them, and re-layouts  5.05 us

commit v1 on v0

v1 whole, which is shorter than its diff:
```python
import functools

import jax
import jax.numpy as jnp
import numpy as np
from jax import lax
from jax.experimental import pallas as pl
from jax.experimental.pallas import tpu as pltpu
from jax.sharding import PartitionSpec as P

F32 = jnp.float32
BF16 = jnp.bfloat16
SPACE = 32
MEMBER = 16
CH = 72
CP = 80
LON = 1440
LP = 1536
PX = 180
KW = 5
KC = KW * CH
KP = 368
PK = 112
SHARES = 27
SR = 40


def lane_index(rows):
    return lax.broadcasted_iota(jnp.int32, (rows, 128), 1)


def packed(wide):
    lane = lane_index(40)
    rest = wide[:, 128:256]
    low = rest[0:40]
    high = jnp.concatenate([rest[40:72], jnp.zeros((8, 128), F32)], axis=0)
    low = jnp.where(lane < PX - 128, low, 0.0)
    high = jnp.where(lane < PX - 128, high, 0.0)
    tail = jnp.where(lane < 64, low, pltpu.roll(high, 64, 1))
    return jnp.concatenate([wide[:, 0:128], tail], axis=0)


def kernel(
    weight_ref,
    pred_ref,
    truth_ref,
    scale_ref,
    hidden_ref,
    filter_ref,
    back_ref,
    kgrad_ref,
    send1,
    recv1,
    scaled,
    trscr,
    fscr,
    send2,
    recv2,
    hid,
    ext,
    stack,
    wst,
    total,
    out_acc,
    ar1_send,
    ar1_recv,
    z1_send,
    z1_recv,
    z2_send,
    z2_recv,
    ar4_send,
    ar4_recv,
    s1_sem,
    r1_sem,
    h1_ssem,
    h1_rsem,
    h2_ssem,
    h2_rsem,
    s2_sem,
    r2_sem,
    a1_ssem,
    a1_rsem,
    z1_ssem,
    z1_rsem,
    z2_ssem,
    z2_rsem,
    a4_ssem,
    a4_rsem,
    near_sem,
    far_sem,
):
    s = lax.axis_index("space")
    m = lax.axis_index("member")
    side = lax.rem(s, 2)
    even = side == 0
    partner = s + 1 - 2 * side
    beyond = s + 2 - 4 * side
    has_prev = s > 0
    has_next = s < SPACE - 1
    has_beyond = jnp.logical_and(beyond >= 0, beyond < SPACE)
    share_id = MEMBER * side + m
    holds_share = share_id < SHARES

    def band(k):
        return lax.rem(s + SPACE + k, SPACE)

    z_low = lax.rem(s // 2, 4)
    z_high = s // 8

    def block_mate(k):
        return 8 * z_high + 2 * lax.rem(z_low + k, 4) + side

    def comb_mate(k):
        return 8 * lax.rem(z_high + k, 4) + 2 * z_low + side

    barrier = pltpu.get_barrier_semaphore()

    def greet(space, member):
        pl.semaphore_signal(barrier, inc=1, device_id={"space": space, "member": member})

    def greet_members(d, _):
        greet(s, lax.rem(m + d, MEMBER))
        return 0

    lax.fori_loop(1, MEMBER, greet_members, 0)

    def greet_bands(d, _):
        n = lax.rem(m + d, MEMBER)

        @pl.when(has_prev)
        def _():
            greet(s - 1, n)

        @pl.when(has_next)
        def _():
            greet(s + 1, n)

        return 0

    lax.fori_loop(0, MEMBER, greet_bands, 0)
    for k in (4, -4):
        greet(band(k), m)
    for k in (1, 2, 3):
        greet(block_mate(k), m)
    pl.semaphore_wait(
        barrier, MEMBER + 4 + jnp.where(has_prev, MEMBER, 0) + jnp.where(has_next, MEMBER, 0)
    )

    def copy1(src, slot, member):
        return pltpu.make_async_remote_copy(
            src_ref=send1.at[src],
            dst_ref=recv1.at[slot],
            send_sem=s1_sem.at[src],
            recv_sem=r1_sem.at[slot],
            device_id={"space": s, "member": member},
        )

    def fields_out(d, _):
        n = lax.rem(m + d, MEMBER)
        row = n // 8
        start = PX * lax.rem(n, 8)
        off = lax.rem(start, 128)
        base = pl.multiple_of(start - off, 128)
        window = pred_ref[row, :, pl.ds(base, 384)].astype(F32)
        wide = pltpu.roll(window, lax.rem(384 - off, 384), 1)[:, 0:256]
        chunk = packed(wide).astype(BF16)

        @pl.when(d < MEMBER)
        def _():
            send1[n] = chunk
            copy1(n, m, n).start()

        @pl.when(d == MEMBER)
        def _():
            recv1[n] = chunk

        return 0

    lax.fori_loop(1, MEMBER + 1, fields_out, 0)

    near_at = 4 - 4 * side
    far_at = 4 * side
    far_at_beyond = 4 * side

    def hidden_near(r, at):
        return pltpu.make_async_remote_copy(
            src_ref=hidden_ref.at[r],
            dst_ref=hid.at[at + r],
            send_sem=h1_ssem.at[r],
            recv_sem=h1_rsem.at[r],
            device_id={"space": partner, "member": m},
        )

    def hidden_far(r, src, dst):
        return pltpu.make_async_remote_copy(
            src_ref=hid.at[src + r],
            dst_ref=hid.at[dst + r],
            send_sem=h2_ssem.at[r],
            recv_sem=h2_rsem.at[r],
            device_id={"space": beyond, "member": m},
        )

    for r in range(2):
        hidden_near(r, far_at).start()
    for k in (4, -4):
        pl.semaphore_signal(near_sem, inc=1, device_id={"space": band(k), "member": m})

    eye = lax.broadcasted_iota(jnp.int32, (CH, CH), 0) == lax.broadcasted_iota(jnp.int32, (CH, CH), 1)
    scale_col = jnp.sum(jnp.where(eye, scale_ref[...], 0.0), axis=1, keepdims=True)
    scale_wide = jnp.broadcast_to(scale_col, (CH, 128))
    scale_pk = packed(jnp.concatenate([scale_wide, scale_wide], axis=1))
    trscr[...] = jnp.zeros_like(trscr)
    trscr[:, 0:PX] = truth_ref[...]
    truth_pk = packed(trscr[...])

    fscr[...] = jnp.zeros_like(fscr)
    wst[...] = jnp.zeros_like(wst)
    for a in range(KW):
        acc = None
        for b in range(KW):
            fscr[0:CH, 0:CH] = filter_ref[a, b].astype(F32)
            part = jnp.concatenate([fscr[...], jnp.zeros((CP, 256), F32)], axis=1)
            if b:
                part = pltpu.roll(part, CH * b, 1)
            acc = part if acc is None else acc + part
        acc = acc.astype(BF16)
        wst[a, 0:CP, :] = acc
        wst[a + 1, CP : 2 * CP, :] = acc
    out_acc[...] = jnp.zeros_like(out_acc)
    for r in range(2):
        hid[2 + r] = hidden_ref[r]

    @pl.when(jnp.logical_not(has_prev))
    def _():
        hid[0] = jnp.zeros((CP, LP), BF16)
        hid[1] = jnp.zeros((CP, LP), BF16)

    @pl.when(jnp.logical_not(has_next))
    def _():
        hid[4] = jnp.zeros((CP, LP), BF16)
        hid[5] = jnp.zeros((CP, LP), BF16)

    def fields_in(d, _):
        n = lax.rem(m + MEMBER - d, MEMBER)

        @pl.when(d < MEMBER)
        def _():
            copy1(n, n, n).wait_recv()

        scaled[n] = scale_pk * recv1[n].astype(F32)
        return 0

    lax.fori_loop(1, MEMBER + 1, fields_in, 0)

    weight = weight_ref[2 * s + m // 8]

    def copy2(kind, src, slot, space, member):
        return pltpu.make_async_remote_copy(
            src_ref=send2.at[src],
            dst_ref=recv2.at[kind, slot],
            send_sem=s2_sem.at[kind, src],
            recv_sem=r2_sem.at[kind, slot],
            device_id={"space": space, "member": member},
        )

    def column_sums(square):
        main = jnp.sum(square[0:CH], axis=0, keepdims=True)
        tail = jnp.sum(square[CH:PK], axis=0, keepdims=True)
        return main, tail + pltpu.roll(tail, 64, 1)

    def spread_out(main, tail):
        return jnp.concatenate(
            [jnp.broadcast_to(main, (CH, 128)), jnp.broadcast_to(tail, (PK - CH, 128))], axis=0
        )

    def gradient(d, _):
        n = lax.rem(m + d, MEMBER)
        y = scaled[n]
        offset = scale_pk * (recv1[n].astype(F32) - truth_pk)
        main, tail = column_sums(offset * offset)
        direct = scale_pk * offset * spread_out(lax.rsqrt(main + 1.0), lax.rsqrt(tail + 1.0))

        def pair(k, mix):
            diff = scaled[k] - y
            main, tail = column_sums(diff * diff)
            return mix + diff * spread_out(lax.rsqrt(main + 1.0), lax.rsqrt(tail + 1.0))

        mix = lax.fori_loop(0, MEMBER, pair, jnp.zeros((PK, 128), F32), unroll=4)
        grad = (weight * (direct + scale_pk * mix * (1.0 / MEMBER))).astype(BF16)
        send2[n] = grad

        @pl.when(d < MEMBER)
        def _():
            copy2(1, n, m, s, n).start()

        @pl.when(d == MEMBER)
        def _():
            recv2[1, n] = grad

        for r in range(2):

            @pl.when(d == 4 + 6 * r)
            def _():
                hidden_near(r, near_at).wait_recv()

                @pl.when(has_beyond)
                def _():
                    hidden_far(r, near_at, far_at_beyond).start()

        return 0

    lax.fori_loop(1, MEMBER + 1, gradient, 0)
    pl.semaphore_wait(near_sem, 2)
    for k in (8, -8):
        pl.semaphore_signal(far_sem, inc=1, device_id={"space": band(k), "member": m})

    def halo_prev(d, _):
        n = lax.rem(m + d, MEMBER)

        @pl.when(has_prev)
        def _():
            copy2(2, n, m, s - 1, n).start()

        return 0

    def halo_next(d, _):
        n = lax.rem(m + d, MEMBER)

        @pl.when(has_next)
        def _():
            copy2(0, n, m, s + 1, n).start()

        return 0

    lax.fori_loop(0, MEMBER, halo_next, 0)
    lax.fori_loop(0, MEMBER, halo_prev, 0)

    def wait_block(kind):
        def one(d, _):
            n = lax.rem(m + MEMBER - d, MEMBER)

            @pl.when(jnp.logical_or(kind != 1, d > 0))
            def _():
                copy2(kind, n, n, s, n).wait_recv()

            return 0

        lax.fori_loop(0, MEMBER, one, 0)

    def rows_ready(kind, half):
        q = 2 * kind + half
        ext[...] = jnp.zeros_like(ext)
        lane = lane_index(PK - CH)
        for k in range(8):
            chunk = recv2[kind, 8 * half + k].astype(F32)
            tail = chunk[CH:PK]
            low = jnp.where(lane < PX - 128, tail, 0.0)
            high = jnp.where(lane < PX - 128, pltpu.roll(tail, 64, 1), 0.0)
            rest = jnp.concatenate([low, high[0:32]], axis=0)
            wide = jnp.concatenate([chunk[0:CH], rest, jnp.zeros((CH, 128), F32)], axis=1)
            start = PX * k + 2
            base, off = start // 128 * 128, start % 128
            ext[:, base : base + 384] += pltpu.roll(wide, off, 1)
        first = ext[:, 0:128]
        last = ext[:, LP - 128 : LP]
        lane = lane_index(CH)
        ext[:, 0:128] = jnp.where(lane < 2, pltpu.roll(last, 96, 1), first)
        ext[:, LP - 128 : LP] = jnp.where(
            jnp.logical_and(lane >= 34, lane < 36), pltpu.roll(first, 32, 1), last
        )

        def piece(p):
            b, g = p // 9, p % 9
            if b == KW:
                return jnp.zeros((8, LP), F32)
            rows = ext[8 * g : 8 * g + 8, :]
            return pltpu.roll(rows, LP - b, 1) if b else rows

        for k in range(KP // 16):
            both = jnp.concatenate([piece(2 * k), piece(2 * k + 1)], axis=0)
            stack[q, 16 * k : 16 * k + 16, :] = both.astype(BF16)

    def block_rows(kind):
        def one(half, _):
            rows_ready(kind, half)
            return 0

        lax.fori_loop(0, 2, one, 0)

    def hidden_terms(kind):
        def one(half, _):
            q = 2 * kind + half
            out_acc[...] += jnp.dot(wst[q, :, 0:KP], stack[q], preferred_element_type=F32)
            return 0

        lax.fori_loop(0, 2, one, 0)

    wait_block(1)
    block_rows(1)

    from_beyond = s - 2 + 4 * side
    has_from = jnp.logical_and(from_beyond >= 0, from_beyond < SPACE)

    @pl.when(has_from)
    def _():
        for r in range(2):
            hidden_far(r, 0, 4 * side).wait_recv()

    def kernel_terms(half):
        rows = hid[half : half + KW].reshape(KW * CP, LP)
        return lax.dot_general(
            rows, stack[2 + half], (((1,), (1,)), ((), ())), preferred_element_type=F32
        )

    product = kernel_terms(0) + kernel_terms(1)
    total[...] = jnp.zeros_like(total)
    for t in range(KW):
        total[CH * t : CH * t + CH, 0:KP] = product[CP * t : CP * t + CH]

    def share_rows(u):
        return pl.ds(pl.multiple_of(SR * lax.rem(u, 9), 8), SR)

    def share_lanes(u):
        return pl.ds(pl.multiple_of(128 * (u // 9), 128), 128)

    def copy_a1(src, slot, space, member):
        return pltpu.make_async_remote_copy(
            src_ref=ar1_send.at[src],
            dst_ref=ar1_recv.at[slot],
            send_sem=a1_ssem.at[src],
            recv_sem=a1_rsem.at[slot],
            device_id={"space": space, "member": member},
        )

    def share_owner(u):
        return s - side + u // MEMBER, lax.rem(u, MEMBER)

    def shares_out(d, _):
        u = lax.rem(share_id + d, 2 * MEMBER)

        @pl.when(u < SHARES)
        def _():
            ar1_send[u] = total[share_rows(u), share_lanes(u)].astype(BF16)
            space, member = share_owner(u)
            copy_a1(u, share_id, space, member).start()

        return 0

    lax.fori_loop(1, 2 * MEMBER, shares_out, 0)

    hidden_terms(1)

    def z1(k, slot):
        return pltpu.make_async_remote_copy(
            src_ref=z1_send,
            dst_ref=z1_recv.at[slot],
            send_sem=z1_ssem.at[k],
            recv_sem=z1_rsem.at[slot],
            device_id={"space": block_mate(k), "member": m},
        )

    def z2(k, slot):
        return pltpu.make_async_remote_copy(
            src_ref=z2_send,
            dst_ref=z2_recv.at[slot],
            send_sem=z2_ssem.at[k],
            recv_sem=z2_rsem.at[slot],
            device_id={"space": comb_mate(k), "member": m},
        )

    pl.semaphore_wait(far_sem, 2)

    @pl.when(holds_share)
    def _():
        def shares_in(d, acc):
            u = lax.rem(share_id + 2 * MEMBER - d, 2 * MEMBER)
            space, member = share_owner(u)
            copy_a1(0, u, space, member).wait_recv()
            return acc + ar1_recv[u].astype(F32)

        own = total[share_rows(share_id), share_lanes(share_id)]
        acc = lax.fori_loop(1, 2 * MEMBER, shares_in, own)
        z1_send[...] = acc
        z1_recv[z_low] = acc
        for k in (1, 2, 3):
            z1(k, z_low).start()

    @pl.when(has_prev)
    def _():
        wait_block(0)
        block_rows(0)
        hidden_terms(0)

    @pl.when(holds_share)
    def _():
        for k in (1, 2, 3):
            z1(k, lax.rem(z_low + k, 4)).wait_recv()
        acc = (z1_recv[0] + z1_recv[1]) + (z1_recv[2] + z1_recv[3])
        z2_send[...] = acc
        z2_recv[z_high] = acc
        for k in (1, 2, 3):
            z2(k, z_high).start()

    @pl.when(has_next)
    def _():
        wait_block(2)
        block_rows(2)
        hidden_terms(2)

    norm = float(1.0 / np.sqrt(np.float32(MEMBER * 2 * SPACE * LON)))

    def copy_a4(u, slot, space, member):
        return pltpu.make_async_remote_copy(
            src_ref=ar4_send,
            dst_ref=ar4_recv.at[slot],
            send_sem=a4_ssem.at[u],
            recv_sem=a4_rsem.at[slot],
            device_id={"space": space, "member": member},
        )

    @pl.when(holds_share)
    def _():
        for k in (1, 2, 3):
            z2(k, lax.rem(z_high + k, 4)).wait_recv()
        acc = (z2_recv[0] + z2_recv[1]) + (z2_recv[2] + z2_recv[3])
        final = (acc * norm).astype(BF16)
        ar4_send[...] = final
        total[share_rows(share_id), share_lanes(share_id)] = final.astype(F32)

        def totals_out(d, _):
            u = lax.rem(share_id + d, 2 * MEMBER)
            space, member = share_owner(u)
            copy_a4(u, share_id, space, member).start()
            return 0

        lax.fori_loop(1, 2 * MEMBER, totals_out, 0)

    back_ref[0] = out_acc[0:CH, 0:LON].astype(BF16)
    back_ref[1] = out_acc[CP : CP + CH, 0:LON].astype(BF16)

    def totals_in(d, _):
        u = lax.rem(share_id + 2 * MEMBER - d, 2 * MEMBER)

        @pl.when(u < SHARES)
        def _():
            space, member = share_owner(u)
            copy_a4(0, u, space, member).wait_recv()
            total[share_rows(u), share_lanes(u)] = ar4_recv[u].astype(F32)

        return 0

    lax.fori_loop(1, 2 * MEMBER, totals_in, 0)
    for a in range(KW):
        for b in range(KW):
            base, off = CH * b // 128 * 128, CH * b % 128
            width = 256 if off + CH > 128 else 128
            part = total[CH * (4 - a) : CH * (5 - a), base : base + width]
            if off:
                part = pltpu.roll(part, width - off, 1)
            kgrad_ref[KW * a + b] = part[:, 0:CH]

    def sent(d, _):
        n = lax.rem(m + d, MEMBER)
        copy1(n, m, n).wait_send()
        copy2(1, n, m, s, n).wait_send()
        return 0

    lax.fori_loop(1, MEMBER, sent, 0)

    def halo_sent(d, _):
        n = lax.rem(m + d, MEMBER)

        @pl.when(has_prev)
        def _():
            copy2(2, n, m, s - 1, n).wait_send()

        @pl.when(has_next)
        def _():
            copy2(0, n, m, s + 1, n).wait_send()

        return 0

    lax.fori_loop(0, MEMBER, halo_sent, 0)

    def shares_sent(d, _):
        u = lax.rem(share_id + d, 2 * MEMBER)
        space, member = share_owner(u)

        @pl.when(u < SHARES)
        def _():
            copy_a1(u, share_id, space, member).wait_send()

        @pl.when(holds_share)
        def _():
            copy_a4(u, share_id, space, member).wait_send()

        return 0

    lax.fori_loop(1, 2 * MEMBER, shares_sent, 0)
    for r in range(2):
        hidden_near(r, far_at).wait_send()

        @pl.when(has_beyond)
        def _():
            hidden_far(r, near_at, far_at_beyond).wait_send()

    @pl.when(holds_share)
    def _():
        for k in (1, 2, 3):
            z1(k, z_low).wait_send()
            z2(k, z_high).wait_send()


def call(weights, pred, truth, scale, hidden, filters):
    vmem = pl.BlockSpec(memory_space=pltpu.VMEM)
    dma = pltpu.SemaphoreType.DMA
    return pl.pallas_call(
        kernel,
        out_shape=(
            jax.ShapeDtypeStruct((2, CH, LON), BF16),
            jax.ShapeDtypeStruct((KW * KW, CH, CH), F32),
        ),
        in_specs=[pl.BlockSpec(memory_space=pltpu.SMEM)] + [vmem] * 5,
        out_specs=(vmem, vmem),
        scratch_shapes=[
            pltpu.VMEM((MEMBER, PK, 128), BF16),
            pltpu.VMEM((MEMBER, PK, 128), BF16),
            pltpu.VMEM((MEMBER, PK, 128), F32),
            pltpu.VMEM((CH, 256), F32),
            pltpu.VMEM((CP, 128), F32),
            pltpu.VMEM((MEMBER, PK, 128), BF16),
            pltpu.VMEM((3, MEMBER, PK, 128), BF16),
            pltpu.VMEM((6, CP, LP), BF16),
            pltpu.VMEM((CH, LP), F32),
            pltpu.VMEM((6, KP, LP), BF16),
            pltpu.VMEM((6, 2 * CP, 384), BF16),
            pltpu.VMEM((KC, 384), F32),
            pltpu.VMEM((2 * CP, LP), F32),
            pltpu.VMEM((2 * MEMBER, SR, 128), BF16),
            pltpu.VMEM((2 * MEMBER, SR, 128), BF16),
            pltpu.VMEM((SR, 128), F32),
            pltpu.VMEM((4, SR, 128), F32),
            pltpu.VMEM((SR, 128), F32),
            pltpu.VMEM((4, SR, 128), F32),
            pltpu.VMEM((SR, 128), BF16),
            pltpu.VMEM((2 * MEMBER, SR, 128), BF16),
            dma((MEMBER,)),
            dma((MEMBER,)),
            dma((2,)),
            dma((2,)),
            dma((2,)),
            dma((2,)),
            dma((3, MEMBER)),
            dma((3, MEMBER)),
            dma((2 * MEMBER,)),
            dma((2 * MEMBER,)),
            dma((4,)),
            dma((4,)),
            dma((4,)),
            dma((4,)),
            dma((2 * MEMBER,)),
            dma((2 * MEMBER,)),
            pltpu.SemaphoreType.REGULAR,
            pltpu.SemaphoreType.REGULAR,
        ],
        compiler_params=pltpu.CompilerParams(
            collective_id=0, has_side_effects=True, vmem_limit_bytes=48 * 1024 * 1024
        ),
    )(weights, pred, truth, scale, hidden, filters)


def body(prediction_maps, truth_analysis, reciprocal_spread, deconv_inputs, filter_tensor):
    rows = 2 * SPACE
    index = np.arange(rows, dtype=np.float64)
    cosine = np.cos((index + 0.5) * (np.pi / rows) - np.pi / 2)
    weights = jnp.asarray((cosine / cosine.mean()).astype(np.float32))
    pred = jnp.pad(jnp.transpose(prediction_maps[0], (1, 0, 2)), ((0, 0), (0, 0), (0, LP - LON)))
    hidden = jnp.pad(
        jnp.transpose(deconv_inputs[0], (1, 0, 2)), ((0, 0), (0, CP - CH), (0, LP - LON))
    )
    back, kgrad = call(
        weights, pred, truth_analysis, reciprocal_spread.reshape(1, CH), hidden, filter_tensor
    )
    return jnp.transpose(back, (1, 0, 2))[None], kgrad.reshape(KW, KW, CH, CH)


def solution(mesh):
    return jax.shard_map(
        body,
        mesh=mesh,
        in_specs=(
            P("member", None, "space", None),
            P(None, ("space", "member")),
            P(),
            P("member", None, "space", None),
            P(),
        ),
        out_specs=(P("member", None, "space", None), P()),
        check_vma=False,
    )
```

time: 95.3 us -> 85.7 us (0.90)
  Pallas kernels: 89.3 us -> 79.6 us
    pallas_call x1, Pallas kernels: 89.3 us -> 79.6 us  [call(): pl.pallas_call(kernel, out_shape=(jax.ShapeDtypeStruct((2, CH, LON), BF16...]
where the time goes in v1:
time: 85.7 us; the launch traced here: 85.5 us
  Pallas kernels  79.6 us (93%)
  local copies, waits for them, and re-layouts  5.12 us (6%)
    pallas_call x1, Pallas kernels, call(): pl.pallas_call(kernel, out_shape=(jax.ShapeDtypeStruct((2, CH, LON), BF16...  79.6 us
    unnamed x14, local copies, waits for them, and re-layouts  5.05 us

profile of v1, /device:TPU:1, one launch (start us, length us, event | category | flops | bytes accessed | tf_op | source)
XLA Modules:
  0.0 85.5 jit_solution(17739215389852674201)
XLA Ops:
  0.6 1.1 %copy.14 = bf16[1,72,2,1440]{3,1,2,0:T(8,128)(2,1)S(1)} copy(bf16[1,72,2,1440]{3,2,1,0:T(2,128)(2,1)} %param.6) | data formatting | bytes 829440 | tf_op args[0]
  1.7 0.0 copy-start.4
  1.7 1.0 %copy-done.4 = bf16[1,72,2,1440]{3,2,1,0:T(2,128)(2,1)S(1)} copy-done((bf16[1,72,2,1440]{3,2,1,0:T(2,128)(2,1)S(1)}, bf16[1,72,2,1440]{3,2,1,0:T(2,128)(2,1)}, u32[]{:S(2)}) %copy-start.4) | copy-done | bytes 414744
  2.8 0.0 copy-start
  2.8 0.0 copy-start.1
  2.8 0.0 copy-start.2
  2.8 0.0 copy-start.3
  2.9 0.9 %copy-done = bf16[5,5,72,72]{3,2,1,0:T(8,128)(2,1)S(1)} copy-done((bf16[5,5,72,72]{3,2,1,0:T(8,128)(2,1)S(1)}, bf16[5,5,72,72]{3,2,1,0:T(8,128)(2,1)}, u32[]{:S(2)}) %copy-start) | copy-done | bytes 259224
  3.8 0.0 copy-done.1
  3.8 0.0 copy-done.2
  3.8 0.0 copy-done.3
  3.8 79.6 %shard_map.77 = (bf16[2,72,1440]{2,1,0:T(8,128)(2,1)S(1)}, f32[25,72,72]{2,1,0:T(8,128)S(1)}) custom-call(f32[64]{0:T(128)S(1)} %copy-done.3, bf16[2,72,1536]{2,1,0:T(8,128)(2,1)S(1)} %pad.8.pred_ref, f32[72,180]{1,0:T(8,128)S(1)} %copy-done.1, f32[1,72]{1,0:T(1,128)S(1)} %bitcast.17, bf16[2,80,1536]{2,1,0:T(8,128)(2,1)S(1)} %pad.9.hidden_ref, ...), custom_call_target="tpu_custom_call" | custom-call | tf_op jit(solution)/shard_map/pallas_call | solution.py:617
  83.4 1.1 %copy.10 = bf16[1,72,2,1440]{3,2,1,0:T(2,128)(2,1)} copy(bf16[1,72,2,1440]{3,1,2,0:T(8,128)(2,1)S(1)} %bitcast.16) | data formatting | bytes 829440
  84.5 0.9 %copy.16 = f32[5,5,72,72]{3,2,1,0:T(8,128)} copy(f32[5,5,72,72]{3,2,1,0:T(8,128)S(1)} %bitcast.15) | data formatting | bytes 1036800
  (3 shorter events, 0.1 us)
Async XLA Ops:
  1.7 1.0 %copy-start.4 = (bf16[1,72,2,1440]{3,2,1,0:T(2,128)(2,1)S(1)}, bf16[1,72,2,1440]{3,2,1,0:T(2,128)(2,1)}, u32[]{:S(2)}) copy-start(bf16[1,72,2,1440]{3,2,1,0:T(2,128)(2,1)} %param.9) | copy-start | bytes 1244164
  2.8 1.0 %copy-start = (bf16[5,5,72,72]{3,2,1,0:T(8,128)(2,1)S(1)}, bf16[5,5,72,72]{3,2,1,0:T(8,128)(2,1)}, u32[]{:S(2)}) copy-start(bf16[5,5,72,72]{3,2,1,0:T(8,128)(2,1)} %filter_ref.1) | copy-start | bytes 777604
  2.8 1.0 %copy-start.1 = (f32[72,180]{1,0:T(8,128)S(1)}, f32[72,180]{1,0:T(8,128)}, u32[]{:S(2)}) copy-start(f32[72,180]{1,0:T(8,128)} %truth_ref.1) | copy-start | bytes 155524
  2.8 1.0 %copy-start.2 = (f32[72]{0:T(128)S(1)}, f32[72]{0:T(128)}, u32[]{:S(2)}) copy-start(f32[72]{0:T(128)} %param.8) | copy-start | bytes 868
  2.8 1.0 %copy-start.3 = (f32[64]{0:T(128)S(1)}, f32[64]{0:T(128)}, u32[]{:S(2)}) copy-start(f32[64]{0:T(128)} %constant.5.clone.weight_ref) | copy-start | bytes 772

commit v2 on v1

--- a/solution.py
+++ b/solution.py
@@ -52,6 +52,9 @@
     send1,
     recv1,
     scaled,
+    target,
+    factor,
+    grads,
     trscr,
     fscr,
     send2,
@@ -86,8 +89,10 @@
     z2_rsem,
     a4_ssem,
     a4_rsem,
-    near_sem,
-    far_sem,
+    span1,
+    span2,
+    span4,
+    span8,
 ):
     s = lax.axis_index("space")
     m = lax.axis_index("member")
@@ -124,27 +129,15 @@
 
     lax.fori_loop(1, MEMBER, greet_members, 0)
 
-    def greet_bands(d, _):
-        n = lax.rem(m + d, MEMBER)
-
-        @pl.when(has_prev)
-        def _():
-            greet(s - 1, n)
-
-        @pl.when(has_next)
-        def _():
-            greet(s + 1, n)
-
-        return 0
-
-    lax.fori_loop(0, MEMBER, greet_bands, 0)
-    for k in (4, -4):
+    for k in (1, -1):
         greet(band(k), m)
-    for k in (1, 2, 3):
-        greet(block_mate(k), m)
-    pl.semaphore_wait(
-        barrier, MEMBER + 4 + jnp.where(has_prev, MEMBER, 0) + jnp.where(has_next, MEMBER, 0)
-    )
+    pl.semaphore_wait(barrier, MEMBER + 1)
+
+    def tell(sem, k):
+        for offset in (k, -k):
+            pl.semaphore_signal(sem, inc=1, device_id={"space": band(offset), "member": m})
+
+    tell(span1, 1)
 
     def copy1(src, slot, member):
         return pltpu.make_async_remote_copy(
@@ -202,8 +195,6 @@
 
     for r in range(2):
         hidden_near(r, far_at).start()
-    for k in (4, -4):
-        pl.semaphore_signal(near_sem, inc=1, device_id={"space": band(k), "member": m})
 
     eye = lax.broadcasted_iota(jnp.int32, (CH, CH), 0) == lax.broadcasted_iota(jnp.int32, (CH, CH), 1)
     scale_col = jnp.sum(jnp.where(eye, scale_ref[...], 0.0), axis=1, keepdims=True)
@@ -240,6 +231,9 @@
         hid[4] = jnp.zeros((CP, LP), BF16)
         hid[5] = jnp.zeros((CP, LP), BF16)
 
+    pl.semaphore_wait(span1, 2)
+    tell(span2, 2)
+
     def fields_in(d, _):
         n = lax.rem(m + MEMBER - d, MEMBER)
 
@@ -247,12 +241,62 @@
         def _():
             copy1(n, n, n).wait_recv()
 
-        scaled[n] = scale_pk * recv1[n].astype(F32)
+        y = scale_pk * recv1[n].astype(F32)
+        scaled[pl.ds(n, PK, stride=2 * MEMBER), :] = y
+        scaled[pl.ds(n + MEMBER, PK, stride=2 * MEMBER), :] = y
         return 0
 
     lax.fori_loop(1, MEMBER + 1, fields_in, 0)
-
-    weight = weight_ref[2 * s + m // 8]
+    pl.semaphore_wait(span2, 2)
+    tell(span4, 4)
+
+    target[...] = scale_pk * truth_pk
+    factor[...] = weight_ref[2 * s + m // 8] * scale_pk
+    turns = MEMBER // 2
+
+    def fields_of(c, turn):
+        return scaled[pl.ds(2 * MEMBER * c + turn, MEMBER), :]
+
+    def squares(c, sums):
+        y = fields_of(c, 0)
+        off = y - target[pl.ds(c, 1), :]
+        new = [sums[0] + off * off]
+        for r in range(1, turns + 1):
+            diff = fields_of(c, r) - y
+            new.append(sums[r] + diff * diff)
+        return tuple(new)
+
+    zeros = tuple(jnp.zeros((MEMBER, 128), F32) for _ in range(turns + 1))
+    main_sums = lax.fori_loop(0, CH, squares, zeros, unroll=4)
+    tail_sums = lax.fori_loop(CH, PK, squares, zeros, unroll=4)
+
+    def inverses(sums, tail):
+        inv = []
+        for v in sums:
+            if tail:
+                v = v + pltpu.roll(v, 64, 1)
+            inv.append(lax.rsqrt(v + 1.0))
+        for r in range(turns + 1, MEMBER):
+            inv.append(pltpu.roll(inv[MEMBER - r], MEMBER - r, 0))
+        return inv
+
+    def mixtures(inv):
+        all_of = functools.reduce(lambda a, b: a + b, inv[1:])
+
+        def one(c, _):
+            y = fields_of(c, 0)
+            mix = inv[1] * fields_of(c, 1)
+            for r in range(2, MEMBER):
+                mix = mix + inv[r] * fields_of(c, r)
+            direct = (y - target[pl.ds(c, 1), :]) * inv[0]
+            value = direct + (mix - y * all_of) * (1.0 / MEMBER)
+            grads[pl.ds(MEMBER * c, MEMBER), :] = value * factor[pl.ds(c, 1), :]
+            return 0
+
+        return one
+
+    lax.fori_loop(0, CH, mixtures(inverses(main_sums, False)), 0, unroll=4)
+    lax.fori_loop(CH, PK, mixtures(inverses(tail_sums, True)), 0, unroll=4)
 
     def copy2(kind, src, slot, space, member):
         return pltpu.make_async_remote_copy(
@@ -263,30 +307,9 @@
             device_id={"space": space, "member": member},
         )
 
-    def column_sums(square):
-        main = jnp.sum(square[0:CH], axis=0, keepdims=True)
-        tail = jnp.sum(square[CH:PK], axis=0, keepdims=True)
-        return main, tail + pltpu.roll(tail, 64, 1)
-
-    def spread_out(main, tail):
-        return jnp.concatenate(
-            [jnp.broadcast_to(main, (CH, 128)), jnp.broadcast_to(tail, (PK - CH, 128))], axis=0
-        )
-
-    def gradient(d, _):
+    def gradients_out(d, _):
         n = lax.rem(m + d, MEMBER)
-        y = scaled[n]
-        offset = scale_pk * (recv1[n].astype(F32) - truth_pk)
-        main, tail = column_sums(offset * offset)
-        direct = scale_pk * offset * spread_out(lax.rsqrt(main + 1.0), lax.rsqrt(tail + 1.0))
-
-        def pair(k, mix):
-            diff = scaled[k] - y
-            main, tail = column_sums(diff * diff)
-            return mix + diff * spread_out(lax.rsqrt(main + 1.0), lax.rsqrt(tail + 1.0))
-
-        mix = lax.fori_loop(0, MEMBER, pair, jnp.zeros((PK, 128), F32), unroll=4)
-        grad = (weight * (direct + scale_pk * mix * (1.0 / MEMBER))).astype(BF16)
+        grad = grads[pl.ds(n, PK, stride=MEMBER), :].astype(BF16)
         send2[n] = grad
 
         @pl.when(d < MEMBER)
@@ -297,22 +320,18 @@
         def _():
             recv2[1, n] = grad
 
-        for r in range(2):
-
-            @pl.when(d == 4 + 6 * r)
-            def _():
-                hidden_near(r, near_at).wait_recv()
-
-                @pl.when(has_beyond)
-                def _():
-                    hidden_far(r, near_at, far_at_beyond).start()
-
-        return 0
-
-    lax.fori_loop(1, MEMBER + 1, gradient, 0)
-    pl.semaphore_wait(near_sem, 2)
-    for k in (8, -8):
-        pl.semaphore_signal(far_sem, inc=1, device_id={"space": band(k), "member": m})
+        return 0
+
+    lax.fori_loop(1, MEMBER + 1, gradients_out, 0)
+    for r in range(2):
+        hidden_near(r, near_at).wait_recv()
+
+        @pl.when(has_beyond)
+        def _():
+            hidden_far(r, near_at, far_at_beyond).start()
+
+    pl.semaphore_wait(span4, 2)
+    tell(span8, 8)
 
     def halo_prev(d, _):
         n = lax.rem(m + d, MEMBER)
@@ -468,7 +487,11 @@
             device_id={"space": comb_mate(k), "member": m},
         )
 
-    pl.semaphore_wait(far_sem, 2)
+    def four(ref):
+        a, b, c, d = (ref[k].astype(F32) for k in range(4))
+        return (a + b) + (c + d)
+
+    pl.semaphore_wait(span8, 2)
 
     @pl.when(holds_share)
     def _():
@@ -479,7 +502,7 @@
             return acc + ar1_recv[u].astype(F32)
 
         own = total[share_rows(share_id), share_lanes(share_id)]
-        acc = lax.fori_loop(1, 2 * MEMBER, shares_in, own)
+        acc = lax.fori_loop(1, 2 * MEMBER, shares_in, own).astype(BF16)
         z1_send[...] = acc
         z1_recv[z_low] = acc
         for k in (1, 2, 3):
@@ -495,7 +518,7 @@
     def _():
         for k in (1, 2, 3):
             z1(k, lax.rem(z_low + k, 4)).wait_recv()
-        acc = (z1_recv[0] + z1_recv[1]) + (z1_recv[2] + z1_recv[3])
+        acc = four(z1_recv).astype(BF16)
         z2_send[...] = acc
         z2_recv[z_high] = acc
         for k in (1, 2, 3):
@@ -522,8 +545,7 @@
     def _():
         for k in (1, 2, 3):
             z2(k, lax.rem(z_high + k, 4)).wait_recv()
-        acc = (z2_recv[0] + z2_recv[1]) + (z2_recv[2] + z2_recv[3])
-        final = (acc * norm).astype(BF16)
+        final = (four(z2_recv) * norm).astype(BF16)
         ar4_send[...] = final
         total[share_rows(share_id), share_lanes(share_id)] = final.astype(F32)
 
@@ -625,7 +647,10 @@
         scratch_shapes=[
             pltpu.VMEM((MEMBER, PK, 128), BF16),
             pltpu.VMEM((MEMBER, PK, 128), BF16),
-            pltpu.VMEM((MEMBER, PK, 128), F32),
+            pltpu.VMEM((2 * MEMBER * PK, 128), F32),
+            pltpu.VMEM((PK, 128), F32),
+            pltpu.VMEM((PK, 128), F32),
+            pltpu.VMEM((MEMBER * PK, 128), F32),
             pltpu.VMEM((CH, 256), F32),
             pltpu.VMEM((CP, 128), F32),
             pltpu.VMEM((MEMBER, PK, 128), BF16),
@@ -638,10 +663,10 @@
             pltpu.VMEM((2 * CP, LP), F32),
             pltpu.VMEM((2 * MEMBER, SR, 128), BF16),
             pltpu.VMEM((2 * MEMBER, SR, 128), BF16),
-            pltpu.VMEM((SR, 128), F32),
-            pltpu.VMEM((4, SR, 128), F32),
-            pltpu.VMEM((SR, 128), F32),
-            pltpu.VMEM((4, SR, 128), F32),
+            pltpu.VMEM((SR, 128), BF16),
+            pltpu.VMEM((4, SR, 128), BF16),
+            pltpu.VMEM((SR, 128), BF16),
+            pltpu.VMEM((4, SR, 128), BF16),
             pltpu.VMEM((SR, 128), BF16),
             pltpu.VMEM((2 * MEMBER, SR, 128), BF16),
             dma((MEMBER,)),
@@ -662,6 +687,8 @@
             dma((2 * MEMBER,)),
             pltpu.SemaphoreType.REGULAR,
             pltpu.SemaphoreType.REGULAR,
+            pltpu.SemaphoreType.REGULAR,
+            pltpu.SemaphoreType.REGULAR,
         ],
         compiler_params=pltpu.CompilerParams(
             collective_id=0, has_side_effects=True, vmem_limit_bytes=48 * 1024 * 1024

time: 85.7 us -> 83.5 us (0.974)
  Pallas kernels: 79.6 us -> 77.5 us
    pallas_call x1, Pallas kernels: 79.6 us -> 77.5 us  [call(): pl.pallas_call(kernel, out_shape=(jax.ShapeDtypeStruct((2, CH, LON), BF16...]
where the time goes in v2:
time: 83.5 us; the launch traced here: 83.3 us
  Pallas kernels  77.5 us (93%)
  local copies, waits for them, and re-layouts  5.12 us (6%)
    pallas_call x1, Pallas kernels, call(): pl.pallas_call(kernel, out_shape=(jax.ShapeDtypeStruct((2, CH, LON), BF16...  77.5 us
    unnamed x14, local copies, waits for them, and re-layouts  5.05 us

profile of v2, /device:TPU:1, one launch (start us, length us, event | category | flops | bytes accessed | tf_op | source)
XLA Modules:
  0.0 83.3 jit_solution(2163649259080998454)
XLA Ops:
  0.6 1.1 %copy.14 = bf16[1,72,2,1440]{3,1,2,0:T(8,128)(2,1)S(1)} copy(bf16[1,72,2,1440]{3,2,1,0:T(2,128)(2,1)} %param.6) | data formatting | bytes 829440 | tf_op args[0]
  1.7 0.0 copy-start.4
  1.7 1.0 %copy-done.4 = bf16[1,72,2,1440]{3,2,1,0:T(2,128)(2,1)S(1)} copy-done((bf16[1,72,2,1440]{3,2,1,0:T(2,128)(2,1)S(1)}, bf16[1,72,2,1440]{3,2,1,0:T(2,128)(2,1)}, u32[]{:S(2)}) %copy-start.4) | copy-done | bytes 414744
  2.8 0.0 copy-start
  2.8 0.0 copy-start.1
  2.8 0.0 copy-start.2
  2.8 0.0 copy-start.3
  2.9 0.9 %copy-done = bf16[5,5,72,72]{3,2,1,0:T(8,128)(2,1)S(1)} copy-done((bf16[5,5,72,72]{3,2,1,0:T(8,128)(2,1)S(1)}, bf16[5,5,72,72]{3,2,1,0:T(8,128)(2,1)}, u32[]{:S(2)}) %copy-start) | copy-done | bytes 259224
  3.8 0.0 copy-done.1
  3.8 0.0 copy-done.2
  3.8 0.0 copy-done.3
  3.8 77.5 %shard_map.77 = (bf16[2,72,1440]{2,1,0:T(8,128)(2,1)S(1)}, f32[25,72,72]{2,1,0:T(8,128)S(1)}) custom-call(f32[64]{0:T(128)S(1)} %copy-done.3, bf16[2,72,1536]{2,1,0:T(8,128)(2,1)S(1)} %pad.8.pred_ref, f32[72,180]{1,0:T(8,128)S(1)} %copy-done.1, f32[1,72]{1,0:T(1,128)S(1)} %bitcast.17, bf16[2,80,1536]{2,1,0:T(8,128)(2,1)S(1)} %pad.9.hidden_ref, ...), custom_call_target="tpu_custom_call" | custom-call | tf_op jit(solution)/shard_map/pallas_call | solution.py:639
  81.3 1.1 %copy.10 = bf16[1,72,2,1440]{3,2,1,0:T(2,128)(2,1)} copy(bf16[1,72,2,1440]{3,1,2,0:T(8,128)(2,1)S(1)} %bitcast.16) | data formatting | bytes 829440
  82.4 0.9 %copy.16 = f32[5,5,72,72]{3,2,1,0:T(8,128)} copy(f32[5,5,72,72]{3,2,1,0:T(8,128)S(1)} %bitcast.15) | data formatting | bytes 1036800
  (3 shorter events, 0.1 us)
Async XLA Ops:
  1.7 1.0 %copy-start.4 = (bf16[1,72,2,1440]{3,2,1,0:T(2,128)(2,1)S(1)}, bf16[1,72,2,1440]{3,2,1,0:T(2,128)(2,1)}, u32[]{:S(2)}) copy-start(bf16[1,72,2,1440]{3,2,1,0:T(2,128)(2,1)} %param.9) | copy-start | bytes 1244164
  2.8 1.0 %copy-start = (bf16[5,5,72,72]{3,2,1,0:T(8,128)(2,1)S(1)}, bf16[5,5,72,72]{3,2,1,0:T(8,128)(2,1)}, u32[]{:S(2)}) copy-start(bf16[5,5,72,72]{3,2,1,0:T(8,128)(2,1)} %filter_ref.1) | copy-start | bytes 777604
  2.8 1.0 %copy-start.1 = (f32[72,180]{1,0:T(8,128)S(1)}, f32[72,180]{1,0:T(8,128)}, u32[]{:S(2)}) copy-start(f32[72,180]{1,0:T(8,128)} %truth_ref.1) | copy-start | bytes 155524
  2.8 1.0 %copy-start.2 = (f32[72]{0:T(128)S(1)}, f32[72]{0:T(128)}, u32[]{:S(2)}) copy-start(f32[72]{0:T(128)} %param.8) | copy-start | bytes 868
  2.8 1.0 %copy-start.3 = (f32[64]{0:T(128)S(1)}, f32[64]{0:T(128)}, u32[]{:S(2)}) copy-start(f32[64]{0:T(128)} %constant.5.clone.weight_ref) | copy-start | bytes 772
